TPU v7x, 512 devices: a whole 4x4x16 slice. The times are simulated.
512 devices in a mesh: dom: 32 (over x, z_hi, core), cuts: 16 (over z_lo, y).
Axes of the slice: x: 4, y: 4, z: 16 (z_hi: 4, z_lo: 4; z = z_hi * 4 + z_lo), core: 2. Of those that a mesh axis runs over, the one named last changes fastest.
Arguments:
- src_table: float32 [131072, 256], P(('dom', 'cuts')), may hold values from -3 to 3
- src_state: float32 [131072], P(('dom', 'cuts')), may hold values from 0.0001 to 0.1
- dst_table: float32 [131072, 256], P(('dom', 'cuts')), may hold values from 0 to 1.2
- dst_state: float32 [131072], P(('dom', 'cuts')), may hold values from 0.0001 to 0.1
- relations: float32 [400, 256], replicated, may hold values from -3 to 3
- rel_state: float32 [400], replicated, may hold values from 0.0001 to 0.1
- src_rows: int32 [2, 262144], P(None, ('dom', 'cuts')), may hold values from 0 to 255
- dst_rows: int32 [2, 262144], P(None, ('dom', 'cuts')), may hold values from 0 to 255
- rel_ids: int32 [2, 262144], P(None, ('dom', 'cuts')), may hold values from 0 to 399
- neg_rows: int32 [2, 32768], P(None, ('dom', 'cuts')), may hold values from 0 to 255
Outputs:
- src_out: float32 [131072, 256], P(('dom', 'cuts'))
- src_state_out: float32 [131072], P(('dom', 'cuts'))
- dst_out: float32 [131072, 256], P(('dom', 'cuts'))
- dst_state_out: float32 [131072], P(('dom', 'cuts'))
- rel_out: float32 [400, 256], replicated
- rel_state_out: float32 [400], replicated
All inputs are finite; a program needn't handle non-finite values.
Results may differ from a plain program's by a relative error of at most 0.0003.
The roundings to bfloat16 on the way count: a program that leaves them out, or rounds other values in their place, can miss the bound.
Values may be sent and summed in bfloat16 or wider, within the bound.
A program may use at most 64 MiB of HBM per device.

v0:
```python
import jax
import jax.numpy as jnp
from jax import lax
from jax.sharding import PartitionSpec as P

learn_rate = 0.1


def shifted(x, axis, by):
    size = lax.axis_size(axis)
    return lax.ppermute(x, axis, [(i, (i + by) % size) for i in range(size)])


def complex_mul(left, right):
    half = left.shape[-1] // 2
    lr, li = (left[..., :half], left[..., half:])
    rr, ri = (right[..., :half], right[..., half:])
    return jnp.concatenate([lr * rr - li * ri, lr * ri + li * rr], axis=-1)


def complex_back(grad_q, other):
    half = grad_q.shape[-1] // 2
    gr, gi = (grad_q[..., :half], grad_q[..., half:])
    orr, oi = (other[..., :half], other[..., half:])
    return jnp.concatenate([gr * orr + gi * oi, -gr * oi + gi * orr], axis=-1)


def adagrad(weights, state, grad):
    state_new = state + jnp.mean(grad * grad, axis=-1)
    return (weights - learn_rate * grad / jnp.sqrt(state_new)[..., None], state_new)


def edge_pass(source, target, rel, sidx, didx, ridx, nidx):
    width = source.shape[1]
    mine = target[nidx].astype(jnp.bfloat16)
    negs = lax.all_gather(mine, "cuts", axis=0, tiled=True)
    total = negs.shape[0]
    edges = sidx.shape[0]
    block = min(512, edges)
    count = edges // block
    svec = source[sidx].reshape(count, block, width)
    tvec = target[didx].reshape(count, block, width)
    rvec = rel[ridx].reshape(count, block, width)

    def step(grad_neg, items):
        s_blk, t_blk, r_blk = items
        qvec = complex_mul(s_blk, r_blk)
        pos = jnp.sum(qvec * t_blk, axis=-1)
        qb = qvec.astype(jnp.bfloat16)
        scores = jnp.dot(qb, negs.T, preferred_element_type=jnp.float32)
        gb = (jax.nn.sigmoid(scores) / total).astype(jnp.bfloat16)
        coef = -jax.nn.sigmoid(-pos)
        grad_q = coef[:, None] * t_blk + jnp.dot(gb, negs, preferred_element_type=jnp.float32)
        grad_t = coef[:, None] * qvec
        grad_neg = grad_neg + jnp.dot(gb.T, qb, preferred_element_type=jnp.float32)
        return (grad_neg, (complex_back(grad_q, r_blk), grad_t, complex_back(grad_q, s_blk)))

    grad_neg, (grad_s, grad_t, grad_r) = lax.scan(
        step, jnp.zeros((total, width), jnp.float32), (svec, tvec, rvec)
    )
    own_neg = lax.psum_scatter(grad_neg, "cuts", scatter_dimension=0, tiled=True)
    gsrc = jnp.zeros_like(source).at[sidx].add(grad_s.reshape(edges, width))
    gdst = jnp.zeros_like(target).at[didx].add(grad_t.reshape(edges, width)).at[nidx].add(own_neg)
    grel = jnp.zeros_like(rel).at[ridx].add(grad_r.reshape(edges, width))
    return (gsrc, gdst, grel)


def shards(
    src_table,
    src_state,
    dst_table,
    dst_state,
    relations,
    rel_state,
    src_rows,
    dst_rows,
    rel_ids,
    neg_rows,
):
    source, source_st = (src_table, src_state)
    target, target_st = (dst_table, dst_state)
    rel, rel_st = (relations, rel_state)
    for rnd in range(2):
        gsrc, gdst, grel = edge_pass(
            source, target, rel, src_rows[rnd], dst_rows[rnd], rel_ids[rnd], neg_rows[rnd]
        )
        source, source_st = adagrad(source, source_st, gsrc)
        target, target_st = adagrad(target, target_st, gdst)
        total = lax.psum(grel, ("dom", "cuts"))
        rel, rel_st = adagrad(rel, rel_st, total)
        if rnd == 0:
            target, target_st = shifted((target, target_st), "dom", lax.axis_size("dom") // 2)
    return (source, source_st, target, target_st, rel, rel_st)


def solution(mesh):
    return jax.shard_map(
        shards,
        mesh=mesh,
        in_specs=(
            P(("dom", "cuts"), None),
            P(("dom", "cuts")),
            P(("dom", "cuts"), None),
            P(("dom", "cuts")),
            P(),
            P(),
            P(None, ("dom", "cuts")),
            P(None, ("dom", "cuts")),
            P(None, ("dom", "cuts")),
            P(None, ("dom", "cuts")),
        ),
        out_specs=(
            P(("dom", "cuts"), None),
            P(("dom", "cuts")),
            P(("dom", "cuts"), None),
            P(("dom", "cuts")),
            P(),
            P(),
        ),
        check_vma=False,
    )
```

profile of v0, /device:TPU:1, one launch (start us, length us, event | category | flops | bytes accessed | tf_op | source)
XLA Modules:
  0.0 1074.6 jit_solution(12723914191142893300)
XLA Ops:
  8.0 0.8 compare_select_fusion.2
  8.8 2.5 gather_fusion
  12.4 1.6 gather_fusion.1
  15.0 1.6 gather_fusion.2
  17.5 0.5 copy-done.27
  18.0 0.7 gather_fusion.3
  18.6 40.6 %all_gather.6 = bf16[1024,256]{1,0:T(8,128)(2,1)S(1)} all-gather(bf16[64,256]{1,0:T(8,128)(2,1)S(1)} %gather_fusion.3), channel_id=1, replica_groups=mesh['dom'=32,'cuts'=16] {'cuts'}, dimensions={0}, use_global_device_ids=true | all-gather | bytes 557056 | tf_op jit(solution)/shard_map/all_gather | solution.py:36
  59.3 0.8 multiply_convert_fusion.1
  60.1 0.5 convolution_add_fusion
  61.4 1.0 copy.36
  62.4 4.5 scatter_custom_fusion.1
  67.0 1.5 fusion.16
  68.8 3.6 scatter_custom_fusion.2
  72.6 3.4 scatter_custom_fusion
  76.3 1.6 gather_fusion.4
  78.2 0.6 pad_clamp_fusion
  78.8 0.6 pad_clamp_fusion.1
  79.4 452.0 %all-reduce.3.cloned.1.call-done = f32[400,256]{1,0:T(8,128)} async-done(((f32[400,256]{1,0:T(8,128)}), f32[400,256]{1,0:T(8,128)}) %all-reduce.3.cloned.1.call-update) | async-done | bytes 409616 | tf_op jit(solution)/shard_map/psum | solution.py:89
  531.4 1.1 multiply_reduce_fusion.3
  532.6 0.6 copy-done.15
  533.2 1.1 divide_subtract_fusion.1
  534.3 1.6 gather_fusion.5
  536.6 1.4 scatter_fusion
  538.1 0.6 fusion.33
  538.7 4.8 collective-permute-start
  543.6 3.7 collective-permute-done
  547.4 0.8 gather_fusion.7
  548.1 39.5 %all_gather.7 = bf16[1024,256]{1,0:T(8,128)(2,1)} all-gather(bf16[64,256]{1,0:T(8,128)(2,1)S(1)} %gather_fusion.7), channel_id=1, replica_groups=mesh['dom'=32,'cuts'=16] {'cuts'}, dimensions={0}, use_global_device_ids=true | all-gather | bytes 557056 | tf_op jit(solution)/shard_map/all_gather | solution.py:36
  587.6 1.6 gather_fusion.6
  589.4 1.9 multiply_convert_fusion
  591.4 0.9 copy-done.12
  592.3 1.3 fusion
  593.6 1.0 multiply_add_fusion.2
  594.8 4.2 scatter_custom_fusion.7
  599.1 1.5 fusion.19
  600.6 0.6 copy-done.35
  601.2 4.4 collective-permute-start.1
  605.9 3.5 scatter_custom_fusion.5
  609.7 3.5 scatter_custom_fusion.4
  613.3 0.6 fusion.32
  613.9 0.8 divide_subtract_fusion.3
  614.7 446.0 %all-reduce.5.cloned.1.call-done = f32[400,256]{1,0:T(8,128)} async-done(((f32[400,256]{1,0:T(8,128)}), f32[400,256]{1,0:T(8,128)}) %all-reduce.5.cloned.1.call-update) | async-done | bytes 409616 | tf_op jit(solution)/shard_map/psum | solution.py:89
  1060.7 1.1 multiply_reduce_fusion.2
  1061.8 0.6 fusion.30
  1062.4 1.9 divide_subtract_fusion
  1064.3 1.4 scatter_fusion.1
  1065.8 0.6 fusion.31
  1066.4 0.8 divide_subtract_fusion.2
  (126 shorter events, 7.0 us)
Async XLA Ops:
  8.0 523.4 %all-reduce.3.cloned.1.call-start = ((), (), s32[]{:S(2)}) async-start(), calls=%async_computation.2 | async-start | bytes 819200 | tf_op jit(solution)/shard_map/psum | solution.py:89
  8.8 67.2 %copy-start.22 = (s32[512,1]{0,1:T(1,128)}, s32[512,1]{0,1:T(1,128)S(1)}, u32[]{:S(2)}) copy-start(s32[512,1]{0,1:T(1,128)S(1)} %get-tuple-element.96) | copy-start | bytes 6148
  11.4 0.7 copy-start.31
  11.4 1.0 copy-start.2
  12.1 66.8 %copy-start.24 = (s32[512,1]{0,1:T(1,128)}, s32[512,1]{0,1:T(1,128)S(1)}, u32[]{:S(2)}) copy-start(s32[512,1]{0,1:T(1,128)S(1)} %get-tuple-element.94) | copy-start | bytes 6148
  14.0 0.7 copy-start.32
  14.0 1.0 copy-start
  14.3 2.5 copy-start.7
  14.7 2.1 copy-start.9
  14.7 64.1 %copy-start.23 = (s32[512,1]{0,1:T(1,128)}, s32[512,1]{0,1:T(1,128)S(1)}, u32[]{:S(2)}) copy-start(s32[512,1]{0,1:T(1,128)S(1)} %get-tuple-element.92) | copy-start | bytes 6148
  16.8 0.7 copy-start.33
  17.5 0.5 copy-start.27
  17.5 60.8 %copy-start.25 = (s32[64]{0:T(128)}, s32[64]{0:T(128)S(1)}, u32[]{:S(2)}) copy-start(s32[64]{0:T(128)S(1)} %get-tuple-element.100) | copy-start | bytes 772
  60.1 1.0 copy-start.8
  60.1 1.0 copy-start.10
  67.0 469.3 %reduce-scatter.3.cloned.1.call-start = ((), (), s32[]{:S(2)}) async-start(), calls=%async_computation.3 | async-start | bytes 1114112 | tf_op jit(solution)/shard_map/reduce_scatter | solution.py:61
  68.5 992.2 %all-reduce.5.cloned.1.call-start = ((), (), s32[]{:S(2)}) async-start(), calls=%async_computation.5 | async-start | bytes 819200 | tf_op jit(solution)/shard_map/psum | solution.py:89
  68.8 7.3 copy-start.29
  68.8 7.3 copy-start.1
  76.1 1.7 copy-start.17
  77.9 455.3 %copy-start.20 = (f32[400]{0:T(512)S(1)}, f32[400]{0:T(512)}, u32[]{:S(2)}) copy-start(f32[400]{0:T(512)} %param.15) | copy-start | bytes 4804
  532.6 0.6 copy-start.15
  535.9 0.7 copy-start.28
  536.1 7.4 copy-start.3
  536.1 1.9 copy-start.34
  536.3 7.3 copy-start.5
  538.7 48.9 %copy-start.19 = (s32[1024]{0:T(1024)S(1)}, s32[1024]{0:T(1024)}, u32[]{:S(2)}) copy-start(s32[1024]{0:T(1024)} %pad_clamp_fusion.1) | copy-start | bytes 12292
  538.7 8.6 collective-permute-start
  591.3 1.0 copy-start.12
  592.3 1.3 copy-start.4
  592.3 1.3 copy-start.6
  599.0 465.3 %reduce-scatter.5.cloned.1.call-start = ((), (), s32[]{:S(2)}) async-start(), calls=%async_computation.4 | async-start | bytes 1114112 | tf_op jit(solution)/shard_map/reduce_scatter | solution.py:61
  600.5 0.7 copy-start.35
  600.5 5.1 copy-start.11
  600.5 8.8 copy-start.13
  600.5 8.8 copy-start.14
  601.2 464.6 %collective-permute-start.1 = (f32[256]{0:T(256)S(1)}, f32[256]{0:T(256)S(1)}, u32[]{:S(2)}, u32[]{:S(2)}) collective-permute-start(f32[256]{0:T(256)S(1)} %copy-done.35), channel_id=1, source_target_pairs={{0,256},{16,272},{32,288},{48,304},{64,320},{80,336},{96,352},{112... | collective-permute-start | bytes 3080 | tf_op jit(solution)/shard_map/ppermute | solution.py:11
  609.4 3.9 copy-start.18
  609.4 3.9 copy-start.30
  609.7 452.2 %copy-start.16 = (f32[400]{0:T(512)S(1)}, f32[400]{0:T(512)}, u32[]{:S(2)}) copy-start(f32[400]{0:T(512)} %copy-done.15) | copy-start | bytes 4804
  609.7 452.2 %copy-start.21 = (f32[400]{0:T(512)S(1)}, f32[400]{0:T(512)}, u32[]{:S(2)}) copy-start(f32[400]{0:T(512)} %param.15) | copy-start | bytes 4804
  613.9 450.4 %copy-start.26 = (s32[64]{0:T(128)S(1)}, s32[64]{0:T(128)}, u32[]{:S(2)}) copy-start(s32[64]{0:T(128)} %copy-done.25) | copy-start | bytes 772
Sparse Core Ops, SparseCore 0:
  67.1 464.3 all-reduce.2
  599.1 461.4 all-reduce.4
Sparse Core Ops, SparseCore 1:
  70.5 85.2 reduce-scatter.2
  602.3 82.2 reduce-scatter.4
where the time goes:
time: 1080 us; the launch traced here: 1070 us
  waiting for transfers between devices  902 us (84%)
  blocking collectives  80.1 us (7%)
  other arithmetic  39 us (4%)
  local copies, waits for them, and re-layouts  20.6 us (2%)
  between operations  16.3 us (2%)
    psum x2, waiting for transfers between devices, shards(): total = lax.psum(grel, ('dom', 'cuts'))  898 us
    all_gather x2, blocking collectives, edge_pass(): negs = lax.all_gather(mine, 'cuts', axis=0, tiled=True)  80.1 us
  transfers between devices with their start and end apart: 6, of which 3 were waited for; matrix products, arithmetic and copies ran while one was open for 3% of the time, Pallas kernels for 0%

commit v1 on v0

v1 whole, which is shorter than its diff:
```python
import functools

import jax
import jax.numpy as jnp
from jax import lax
from jax.experimental import pallas as pl
from jax.experimental.pallas import tpu as pltpu
from jax.sharding import PartitionSpec as P

RATE = 0.1
MESH = pl.DeviceIdType.MESH
f32, bf16, i32 = jnp.float32, jnp.bfloat16, jnp.int32

AG_Z, AG_Y, AG_F = 0, 3, 6
RS_Y, RS_Z = 15, 27
MOVE, PAIR_A, ZL_A, ZH, ZL_B, PAIR_B = 30, 32, 33, 36, 39, 42
XY_A, XY_B = 43, 59
SEMS = 75


def split2(x):
    hi = x.astype(bf16)
    return hi, (x - hi.astype(f32)).astype(bf16)


def columns(row):
    return jnp.broadcast_to(row, (128, row.shape[1])).T


def pick(col_idx, width):
    lane = lax.broadcasted_iota(i32, col_idx.shape, 1)
    parts = [jnp.where(col_idx == lane + 128 * j, 1.0, 0.0) for j in range(width // 128)]
    return jnp.concatenate(parts, axis=1).astype(bf16)


def spread(row_idx, width):
    at = lax.broadcasted_iota(i32, (width, row_idx.shape[1]), 0)
    return jnp.where(at == row_idx, 1.0, 0.0).astype(bf16)


def exact_dot(ones, x):
    wide = x.shape[1]
    out = jnp.dot(ones, jnp.concatenate(split2(x), axis=1), preferred_element_type=f32)
    return out[:, :wide] + out[:, wide:]


def back(grad, other):
    h = grad.shape[1] // 2
    gr, gi, orr, oi = grad[:, :h], grad[:, h:], other[:, :h], other[:, h:]
    return jnp.concatenate([gr * orr + gi * oi, gi * orr - gr * oi], axis=1)


def adagrad(w, state, g):
    state = state + jnp.sum(g * g, axis=1, keepdims=True) * (1.0 / g.shape[1])
    scale = RATE / jnp.sqrt(state)
    return w - g * jnp.concatenate([scale] * (g.shape[1] // 128), axis=1), state


def kernel(
    s_in, ss_in, t_in, ts_in, r_in, rs_in, sidx, didx, ridx, nidx,
    s_out, ss_out, t_out, ts_out, r_out, rs_out,
    negs, dn_f, dn_b, rs_y, z_b, rs_z, t_new, ts_new, t_got, ts_got,
    gr, pair, part, xy, piece, zl, tile, zh, done,
    s_tab, s_st, t_st, r_tab, r_st, q_v, t_v, r_v, s_v, dq,
    ssem, rsem,
):
    dom, cuts = lax.axis_index("dom"), lax.axis_index("cuts")
    x, z_hi, core = dom // 8, (dom // 2) % 4, dom % 2
    z_lo, y = cuts // 4, cuts % 4
    spot = x * 4 + y
    rels = r_in.shape[0]
    waits = []

    def device(x_=None, z_hi_=None, core_=None, z_lo_=None, y_=None):
        a = x if x_ is None else x_
        b = z_hi if z_hi_ is None else z_hi_
        c = core if core_ is None else core_
        d = z_lo if z_lo_ is None else z_lo_
        e = y if y_ is None else y_
        return (a * 8 + b * 2 + c, d * 4 + e)

    def hop(v, o):
        return (v + o) % 4

    def at_spot(o):
        p = (spot + o) % 16
        return p, device(x_=p // 4, y_=p % 4)

    def remote(k, n, src, dst, dev):
        return pltpu.make_async_remote_copy(
            src_ref=src, dst_ref=dst, send_sem=ssem.at[k, n], recv_sem=rsem.at[k, n],
            device_id=dev, device_id_type=MESH,
        )

    def send(*args):
        copy = remote(*args)
        copy.start()
        waits.append(copy)
        return copy

    other = device(core_=1 - core)
    across = device(x_=hop(x, 2))

    barrier = pltpu.get_barrier_semaphore()

    def greet(o, _):
        pl.semaphore_signal(barrier, inc=1, device_id=at_spot(o)[1], device_id_type=MESH)
        return 0

    lax.fori_loop(1, 16, greet, 0)
    for o in (1, 2, 3):
        pl.semaphore_signal(barrier, inc=1, device_id=device(z_lo_=hop(z_lo, o)), device_id_type=MESH)
        pl.semaphore_signal(barrier, inc=1, device_id=device(z_hi_=hop(z_hi, o)), device_id_type=MESH)
    pl.semaphore_signal(barrier, inc=1, device_id=other, device_id_type=MESH)

    ncol = columns(nidx[...])
    half = nidx.shape[1] // 2
    n_rows = nidx.shape[1] // 2

    def my_negs(k, table):
        ones = pick(ncol[k * half : (k + 1) * half], table.shape[0])
        negs[k, z_lo, y] = jnp.dot(ones, table.astype(bf16), preferred_element_type=f32).astype(bf16)

    def send_negs(k):
        own = negs.at[k, z_lo, y]
        for o in (1, 2, 3):
            send(k, AG_Z + o - 1, own, own, device(z_lo_=hop(z_lo, o)))
        for o in (1, 2, 3):
            send(k, AG_Y + o - 1, own, own, device(y_=hop(y, o)))

    def forward_negs(k):
        for o in (1, 2, 3):
            block = negs.at[k, hop(z_lo, 4 - o), y]
            remote(k, AG_Z + o - 1, block, block, across).wait_recv()
            for p in (1, 2, 3):
                send(k, AG_F + 3 * (o - 1) + p - 1, block, block, device(y_=hop(y, p)))

    def wait_group(k, o):
        first = AG_Y if o == 0 else AG_F + 3 * (o - 1)
        for p in (1, 2, 3):
            block = negs.at[k, hop(z_lo, 4 - o), hop(y, 4 - p)]
            remote(k, first + p - 1, block, block, across).wait_recv()

    def gather_st(k, table):
        s_v[...] = exact_dot(pick(columns(sidx[k : k + 1, :]), 256), s_tab[...])
        t_v[...] = exact_dot(pick(columns(didx[k : k + 1, :]), 256), table)

    def gather_r(k):
        r_v[...] = exact_dot(pick(columns(ridx[k : k + 1, :]), 512), r_tab[...])

    def edges(k):
        s, r = s_v[...], r_v[...]
        h = s.shape[1] // 2
        sr, si, rr, ri = s[:, :h], s[:, h:], r[:, :h], r[:, h:]
        q = jnp.concatenate([sr * rr - si * ri, sr * ri + si * rr], axis=1)
        q_v[...] = q.astype(bf16)
        t = t_v[...]
        coef = -jax.nn.sigmoid(-jnp.sum(q * t, axis=1, keepdims=True))
        dq[...] = coef * t
        return exact_dot(spread(didx[k : k + 1, :], 256), coef * q)

    def group(k, o):
        at = hop(z_lo, 4 - o)
        block = negs[k, at].reshape(4 * n_rows, 256)
        qb = q_v[...]
        scores = lax.dot_general(qb, block, (((1,), (1,)), ((), ())), preferred_element_type=f32)
        gb = (jax.nn.sigmoid(scores) * (1.0 / (16 * n_rows))).astype(bf16)
        dq[...] += jnp.dot(gb, block, preferred_element_type=f32)
        dn = lax.dot_general(gb, qb, (((0,), (0,)), ((), ())), preferred_element_type=f32)
        dn_f[k, at] = dn.reshape(4, n_rows, 256)
        dn_b[k, at] = dn.astype(bf16).reshape(4, n_rows, 256)
        for p in (1, 2, 3):
            to = hop(y, p)
            send(k, RS_Y + 3 * o + p - 1, dn_b.at[k, at, to], rs_y.at[k, at, p], device(y_=to))

    def scatter_y(k):
        for o in (3, 2, 1, 0):
            at = hop(z_lo, 4 - o)
            total = dn_f[k, at, y]
            for p in (1, 2, 3):
                got = rs_y.at[k, at, p]
                remote(k, RS_Y + 3 * o + p - 1, got, got, across).wait_recv()
                total = total + rs_y[k, at, p].astype(f32)
            if o:
                z_b[k, o] = total.astype(bf16)
                send(k, RS_Z + o - 1, z_b.at[k, o], rs_z.at[k, o], device(z_lo_=at))
            else:
                own = total
        return own

    def scatter_z(k, total):
        for o in (1, 2, 3):
            got = rs_z.at[k, o]
            remote(k, RS_Z + o - 1, got, got, across).wait_recv()
            total = total + rs_z[k, o].astype(f32)
        return total

    def own_grad_t(k, total):
        return exact_dot(spread(nidx[:, k * half : (k + 1) * half], 256), total)

    def finish_edges(k):
        d = dq[...]
        dr = back(d, s_v[...])
        total = exact_dot(spread(ridx[k : k + 1, :], 512), dr)
        gr[k, 0] = total[:, :128].reshape(16, 32, 128)
        gr[k, 1] = total[:, 128:].reshape(16, 32, 128)
        send(k, PAIR_A, gr.at[k, 1 - core], pair.at[k], other)

    def finish_s(k):
        ds = back(dq[...], r_v[...])
        g = exact_dot(spread(sidx[k : k + 1, :], 256), ds)
        s_tab[...], s_st[...] = adagrad(s_tab[...], s_st[...], g)

    def rel_pair(k):
        remote(k, PAIR_A, pair.at[k], pair.at[k], other).wait_recv()
        part[k] = gr[k, core] + pair[k]

        def one(o, _):
            p, dev = at_spot(o)
            remote(k, XY_A + o, part.at[k, p], xy.at[k, o], dev).start()
            return 0

        lax.fori_loop(1, 16, one, 0)

    def rel_xy(k):
        total = part[k, spot]
        for o in range(1, 16):
            remote(k, XY_A + o, xy.at[k, o], xy.at[k, o], across).wait_recv()
            total = total + xy[k, o]
        piece[k] = total.reshape(4, 8, 128)
        for o in (1, 2, 3):
            to = hop(z_lo, o)
            send(k, ZL_A + o - 1, piece.at[k, to], zl.at[k, o], device(z_lo_=to))

    def rel_zl(k):
        total = piece[k, z_lo]
        for o in (1, 2, 3):
            remote(k, ZL_A + o - 1, zl.at[k, o], zl.at[k, o], across).wait_recv()
            total = total + zl[k, o]
        zh[k, z_hi] = total
        own = zh.at[k, z_hi]
        for o in (1, 2, 3):
            send(k, ZH + o - 1, own, own, device(z_hi_=hop(z_hi, o)))

    def rel_zh(k):
        for o in (1, 2, 3):
            got = zh.at[k, hop(z_hi, 4 - o)]
            remote(k, ZH + o - 1, got, got, across).wait_recv()
        total = zh[k, 0] + zh[k, 1] + zh[k, 2] + zh[k, 3]
        done[k, core, spot, z_lo] = total
        own = done.at[k, core, spot, z_lo]
        for o in (1, 2, 3):
            send(k, ZL_B + o - 1, own, own, device(z_lo_=hop(z_lo, o)))

    def rel_back(k):
        for o in (1, 2, 3):
            got = done.at[k, core, spot, hop(z_lo, 4 - o)]
            remote(k, ZL_B + o - 1, got, got, across).wait_recv()
        own = done.at[k, core, spot]

        def one(o, _):
            remote(k, XY_B + o, own, own, at_spot(o)[1]).start()
            return 0

        lax.fori_loop(1, 16, one, 0)

    def rel_fill(k):
        def one(o, _):
            got = done.at[k, core, (spot + 16 - o) % 16]
            remote(k, XY_B + o, got, got, across).wait_recv()
            return 0

        lax.fori_loop(1, 16, one, 0)
        send(k, PAIR_B, done.at[k, core], done.at[k, core], other)

    def rel_update(k):
        got = done.at[k, 1 - core]
        remote(k, PAIR_B, got, got, other).wait_recv()
        g = jnp.concatenate([done[k, 0].reshape(512, 128), done[k, 1].reshape(512, 128)], axis=1)
        r_tab[...], r_st[...] = adagrad(r_tab[...], r_st[...], g)

    my_negs(0, t_in[...])
    pl.semaphore_wait(barrier, 22)
    send_negs(0)

    s_tab[...] = s_in[...]
    s_st[...] = columns(ss_in[...])
    t_st[...] = columns(ts_in[...])
    r_tab[...] = jnp.zeros_like(r_tab)
    r_tab[:rels] = r_in[...]
    r_st[...] = jnp.ones_like(r_st)
    r_st[:rels] = columns(rs_in[...])[:rels]
    gather_st(0, t_in[...])
    forward_negs(0)
    gather_r(0)
    g_t = edges(0)
    for o in range(4):
        wait_group(0, o)
        group(0, o)
    finish_edges(0)
    own = scatter_y(0)
    rel_pair(0)
    finish_s(0)
    own = scatter_z(0, own)
    new, state = adagrad(t_in[...], t_st[...], g_t + own_grad_t(0, own))
    t_new[...] = new
    ts_new[...] = state.T[:8]
    send(0, MOVE, t_new, t_got, across)
    send(0, MOVE + 1, ts_new, ts_got, across)
    rel_xy(0)
    rel_zl(0)
    rel_zh(0)
    remote(0, MOVE, t_got, t_got, across).wait_recv()
    my_negs(1, t_got[...])
    send_negs(1)
    rel_back(0)
    remote(0, MOVE + 1, ts_got, ts_got, across).wait_recv()
    t_st[...] = columns(ts_got[:1, :])
    gather_st(1, t_got[...])
    rel_fill(0)
    forward_negs(1)
    rel_update(0)

    gather_r(1)
    g_t = edges(1)
    for o in range(4):
        wait_group(1, o)
        group(1, o)
    finish_edges(1)
    own = scatter_y(1)
    rel_pair(1)
    finish_s(1)
    s_out[...] = s_tab[...]
    ss_out[...] = s_st[...].T[:1]
    own = scatter_z(1, own)
    new, state = adagrad(t_got[...], t_st[...], g_t + own_grad_t(1, own))
    t_out[...] = new
    ts_out[...] = state.T[:1]
    rel_xy(1)
    rel_zl(1)
    rel_zh(1)
    rel_back(1)
    rel_fill(1)
    rel_update(1)
    r_out[...] = r_tab[:rels]
    rs_out[...] = r_st[...].T[:1, :rels]

    for copy in waits:
        copy.wait_send()
    for k in range(2):
        def one(o, _):
            p, dev = at_spot(o)
            remote(k, XY_A + o, part.at[k, p], xy.at[k, o], dev).wait_send()
            own = done.at[k, core, spot]
            remote(k, XY_B + o, own, own, dev).wait_send()
            return 0

        lax.fori_loop(1, 16, one, 0)


def shards(src_table, src_state, dst_table, dst_state, relations, rel_state, src_rows, dst_rows, rel_ids, neg_rows):
    rows, d = src_table.shape
    rels, edges, n = relations.shape[0], src_rows.shape[1], neg_rows.shape[1]
    vm = pltpu.VMEM
    out = pl.pallas_call(
        kernel,
        out_shape=[
            jax.ShapeDtypeStruct((rows, d), f32),
            jax.ShapeDtypeStruct((1, rows), f32),
            jax.ShapeDtypeStruct((rows, d), f32),
            jax.ShapeDtypeStruct((1, rows), f32),
            jax.ShapeDtypeStruct((rels, d), f32),
            jax.ShapeDtypeStruct((1, rels), f32),
        ],
        in_specs=[pl.BlockSpec(memory_space=vm)] * 10,
        out_specs=[pl.BlockSpec(memory_space=vm)] * 6,
        scratch_shapes=[
            vm((2, 4, 4, n, d), bf16),
            vm((2, 4, 4, n, d), f32),
            vm((2, 4, 4, n, d), bf16),
            vm((2, 4, 4, n, d), bf16),
            vm((2, 4, n, d), bf16),
            vm((2, 4, n, d), bf16),
            vm((rows, d), f32),
            vm((8, rows), f32),
            vm((rows, d), f32),
            vm((8, rows), f32),
            vm((2, 2, 16, 32, 128), f32),
            vm((2, 16, 32, 128), f32),
            vm((2, 16, 32, 128), f32),
            vm((2, 16, 32, 128), f32),
            vm((2, 4, 8, 128), f32),
            vm((2, 4, 8, 128), f32),
            vm((2, 8, 128), f32),
            vm((2, 4, 8, 128), f32),
            vm((2, 2, 16, 4, 8, 128), f32),
            vm((rows, d), f32),
            vm((rows, 128), f32),
            vm((rows, 128), f32),
            vm((512, d), f32),
            vm((512, 128), f32),
            vm((edges, d), bf16),
            vm((edges, d), f32),
            vm((edges, d), f32),
            vm((edges, d), f32),
            vm((edges, d), f32),
            pltpu.SemaphoreType.DMA((2, SEMS)),
            pltpu.SemaphoreType.DMA((2, SEMS)),
        ],
        compiler_params=pltpu.CompilerParams(
            collective_id=0, has_side_effects=True, vmem_limit_bytes=48 * 1024 * 1024
        ),
    )(
        src_table, src_state.reshape(1, rows), dst_table, dst_state.reshape(1, rows),
        relations, rel_state.reshape(1, rels), src_rows, dst_rows, rel_ids, neg_rows.reshape(1, 2 * n),
    )
    s, ss, t, ts, r, rs = out
    return s, ss.reshape(rows), t, ts.reshape(rows), r, rs.reshape(rels)


def solution(mesh):
    both = ("dom", "cuts")
    return jax.shard_map(
        shards,
        mesh=mesh,
        in_specs=(P(both, None), P(both), P(both, None), P(both), P(), P()) + (P(None, both),) * 4,
        out_specs=(P(both, None), P(both), P(both, None), P(both), P(), P()),
        check_vma=False,
    )
```

time: 1080 us -> 116 us (0.11)
  waiting for transfers between devices: 902 us -> 0 us
  Pallas kernels: 0 us -> 105 us
  blocking collectives: 80.1 us -> 0 us
  other arithmetic: 39 us -> 0 us
  between operations: 16.3 us -> 0.68 us
  local copies, waits for them, and re-layouts: 20.6 us -> 9.6 us
    psum x2 -> x0, waiting for transfers between devices: 898 us -> none  [shards(): total = lax.psum(grel, ('dom', 'cuts'))]
    pallas_call x0 -> x1, Pallas kernels: none -> 105 us  [shards(): pl.pallas_call(kernel, out_shape=[jax.ShapeDtypeStruct((rows, d), f32), j...]
    all_gather x2 -> x0, blocking collectives: 80.1 us -> none  [edge_pass(): negs = lax.all_gather(mine, 'cuts', axis=0, tiled=True)]
    scatter-add x8 -> x0, other arithmetic: 25.3 us -> none  [the longest x4 9.77 us: edge_pass(): jnp.zeros_like(target).at[didx].add(grad_t.reshape(edges, width)).at[nidx]]
    gather x10 -> x0, local copies, waits for them, and re-layouts: 12.2 us -> none  [the longest x2 4.09 us: edge_pass(): svec = source[sidx].reshape(count, block, width)]
  transfers between devices with their start and end apart: 6 -> 0, of which waited for: 3 -> 0; matrix products, arithmetic and copies ran while one was open for 3% -> 0% of each run, Pallas kernels for 0% -> 0%
where the time goes in v1:
time: 116 us
  Pallas kernels  105 us (91%)
  local copies, waits for them, and re-layouts  9.6 us (8%)
    pallas_call x1, Pallas kernels, shards(): pl.pallas_call(kernel, out_shape=[jax.ShapeDtypeStruct((rows, d), f32), j...  105 us
    unnamed x24, local copies, waits for them, and re-layouts  8.82 us

profile of v1, /device:TPU:1, one launch (start us, length us, event | category | flops | bytes accessed | tf_op | source)
XLA Modules:
  0.0 115.7 jit_solution(9271950198860479484)
XLA Ops:
  0.6 0.0 copy-start.3
  0.6 0.0 copy-start.6
  0.7 0.0 copy-start.7
  0.7 0.8 reshape.36.nidx
  1.4 0.0 copy-done.3
  1.4 0.0 copy-done.6
  1.4 0.0 copy-done.7
  1.4 0.0 copy-start
  1.5 1.0 copy-done
  2.5 0.0 copy-start.1
  2.5 0.9 copy-done.1
  3.4 0.0 copy-start.2
  3.4 0.9 copy-done.2
  4.4 0.0 copy-start.4
  4.4 0.7 copy-done.4
  5.0 0.0 copy-start.5
  5.0 0.7 copy-done.5
  5.7 0.0 copy-start.8
  5.7 0.7 copy-done.8
  6.4 105.4 %shard_map.145 = (f32[256,256]{1,0:T(8,128)S(1)}, f32[1,256]{1,0:T(1,128)S(1)}, f32[256,256]{1,0:T(8,128)S(1)}, f32[1,256]{1,0:T(1,128)S(1)}, f32[400,256]{1,0:T(8,128)S(1)}, /*index=5*/f32[1,400]{1,0:T(1,128)S(1)}) custom-call(f32[256,256]{1,0:T(8,128)S(1)} %copy-done.1, f32[1,256]{1,0:T(1,128)S(1)} %bitcast.8, f32[256,256]{1,0:T(8,128)S(1)} %copy-done.2, ...), custom_call_target="tpu_custom_call" | custom-call | tf_op jit(solution)/shard_map/pallas_call | solution.py:365
  111.8 0.7 copy.22
  112.5 0.6 copy.23
  113.1 0.7 copy.24
  113.8 0.6 copy.25
  114.3 0.8 copy.26
  115.1 0.6 copy.27
Async XLA Ops:
  0.6 0.8 copy-start.3
  0.6 0.8 copy-start.6
  0.7 0.8 copy-start.7
  1.4 1.0 copy-start
  2.5 0.9 copy-start.1
  3.4 0.9 copy-start.2
  4.4 0.7 copy-start.4
  5.0 0.7 copy-start.5
  5.7 0.7 copy-start.8

commit v2 on v1

v2 whole, which is shorter than its diff:
```python
import functools

import jax
import jax.numpy as jnp
from jax import lax
from jax.experimental import pallas as pl
from jax.experimental.pallas import tpu as pltpu
from jax.sharding import PartitionSpec as P

RATE = 0.1
MESH = pl.DeviceIdType.MESH
f32, bf16, i32 = jnp.float32, jnp.bfloat16, jnp.int32

AG_Z, AG_Y, AG_F = 0, 3, 6
RS_Y, RS_Z = 15, 27
IDX, EARLY, LATE, PAIR_A, ZL_B, PAIR_B = 30, 31, 33, 35, 36, 39
XY_A, Z_A, XY_B = 43, 59, 75
SEMS = 139


def split2(x):
    hi = x.astype(bf16)
    return hi, (x - hi.astype(f32)).astype(bf16)


def columns(row):
    return jnp.broadcast_to(row, (128, row.shape[1])).T


def pick(col_idx, width):
    lane = lax.broadcasted_iota(i32, col_idx.shape, 1)
    parts = [jnp.where(col_idx == lane + 128 * j, 1.0, 0.0) for j in range(width // 128)]
    return jnp.concatenate(parts, axis=1).astype(bf16)


def spread(row_idx, width):
    at = lax.broadcasted_iota(i32, (width, row_idx.shape[1]), 0)
    return jnp.where(at == row_idx, 1.0, 0.0).astype(bf16)


def exact_dot(ones, x):
    wide = x.shape[1]
    out = jnp.dot(ones, jnp.concatenate(split2(x), axis=1), preferred_element_type=f32)
    return out[:, :wide] + out[:, wide:]


def back(grad, other):
    h = grad.shape[1] // 2
    gr, gi, orr, oi = grad[:, :h], grad[:, h:], other[:, :h], other[:, h:]
    return jnp.concatenate([gr * orr + gi * oi, gi * orr - gr * oi], axis=1)


def adagrad(w, state, g):
    state = state + jnp.sum(g * g, axis=1, keepdims=True) * (1.0 / g.shape[1])
    scale = RATE / jnp.sqrt(state)
    return w - g * jnp.concatenate([scale] * (g.shape[1] // 128), axis=1), state


def kernel(
    s_hbm, ss_hbm, t_hbm, ts_hbm, r_hbm, rs_hbm, sidx_hbm, didx_hbm, ridx_hbm, nidx_hbm,
    s_tab, ss_out, t_out, ts_out, r_out, rs_out,
    ss_in, t_in, ts_in, r_tab, rs_in, sidx, didx, ridx, nidx,
    negs, dn_f, dn_b, rs_y, z_b, rs_z,
    n_f, n_got, t_soon, ts_soon, t_got, ts_got, late, late_st, late_got, late_st_got,
    gr, pair, part, xy, piece, zs, done,
    s_st, t_st, t_tab, r_st, at_s, at_t, at_r, pick_r, g_r,
    q_v, t_v, r_v, s_v, dq,
    in_sem, ssem, rsem,
):
    dom, cuts = lax.axis_index("dom"), lax.axis_index("cuts")
    x, z_hi, core = dom // 8, (dom // 2) % 4, dom % 2
    z_lo, y = cuts // 4, cuts % 4
    spot, z = x * 4 + y, z_hi * 4 + z_lo
    rels = r_hbm.shape[0]
    n = nidx.shape[1]
    waits = []

    def device(x_=None, z_=None, core_=None, y_=None):
        a = x if x_ is None else x_
        b = z if z_ is None else z_
        c = core if core_ is None else core_
        d = y if y_ is None else y_
        return (a * 8 + (b // 4) * 2 + c, (b % 4) * 4 + d)

    def hop(v, o):
        return (v + o) % 4

    def z_line(o):
        return device(z_=z_hi * 4 + hop(z_lo, o))

    def at_spot(o):
        p = (spot + o) % 16
        return p, device(x_=p // 4, y_=p % 4)

    def at_z(o):
        p = (z + o) % 16
        return p, device(z_=p)

    def remote(k, n, src, dst, dev):
        return pltpu.make_async_remote_copy(
            src_ref=src, dst_ref=dst, send_sem=ssem.at[k, n], recv_sem=rsem.at[k, n],
            device_id=dev, device_id_type=MESH,
        )

    def send(*args):
        copy = remote(*args)
        copy.start()
        waits.append(copy)

    def recv(k, n, ref):
        remote(k, n, ref, ref, other).wait_recv()

    other = device(core_=1 - core)
    across = device(x_=hop(x, 2))

    barrier = pltpu.get_barrier_semaphore()

    def greet(o, _):
        pl.semaphore_signal(barrier, inc=1, device_id=at_z(o)[1], device_id_type=MESH)
        pl.semaphore_signal(barrier, inc=1, device_id=at_spot(o)[1], device_id_type=MESH)
        return 0

    lax.fori_loop(1, 16, greet, 0)
    pl.semaphore_signal(barrier, inc=1, device_id=other, device_id_type=MESH)

    ins = [
        (nidx_hbm, nidx), (t_hbm, t_in), (didx_hbm, didx), (sidx_hbm, sidx), (s_hbm, s_tab),
        (ridx_hbm, ridx), (r_hbm, r_tab.at[pl.ds(0, rels)]), (ts_hbm, ts_in), (ss_hbm, ss_in), (rs_hbm, rs_in),
    ]
    loads = [pltpu.make_async_copy(a, b, in_sem.at[i]) for i, (a, b) in enumerate(ins)]
    for load in loads:
        load.start()

    def neg_row(k):
        return nidx[k : k + 1, :]

    def my_negs(k, table):
        row = jnp.concatenate([neg_row(k), neg_row(k)], axis=1)
        ones = pick(columns(row)[:n], table.shape[0])
        negs[k, z_lo, y] = jnp.dot(ones, table.astype(bf16), preferred_element_type=f32).astype(bf16)

    def send_negs(k):
        own = negs.at[k, z_lo, y]
        for o in (1, 2, 3):
            send(k, AG_Z + o - 1, own, own, z_line(o))
        for o in (1, 2, 3):
            send(k, AG_Y + o - 1, own, own, device(y_=hop(y, o)))

    def forward_negs(k):
        for o in (1, 2, 3):
            block = negs.at[k, hop(z_lo, 4 - o), y]
            recv(k, AG_Z + o - 1, block)
            for p in (1, 2, 3):
                send(k, AG_F + 3 * (o - 1) + p - 1, block, block, device(y_=hop(y, p)))

    def wait_group(k, o):
        first = AG_Y if o == 0 else AG_F + 3 * (o - 1)
        for p in (1, 2, 3):
            recv(k, first + p - 1, negs.at[k, hop(z_lo, 4 - o), hop(y, 4 - p)])

    def place_edges(k):
        at_s[k] = spread(sidx[k : k + 1, :], 256)
        at_t[k] = spread(didx[k : k + 1, :], 256)
        at_r[k] = spread(ridx[k : k + 1, :], rels)
        pick_r[k] = pick(columns(ridx[k : k + 1, :]), 512)

    def gather_s(k):
        s_v[...] = exact_dot(pick(columns(sidx[k : k + 1, :]), 256), s_tab[...])

    def gather_t(k, table):
        t_v[...] = exact_dot(pick(columns(didx[k : k + 1, :]), 256), table)

    def gather_r(k):
        r_v[...] = exact_dot(pick_r[k], r_tab[...])

    def edges(k):
        s, r = s_v[...], r_v[...]
        h = s.shape[1] // 2
        sr, si, rr, ri = s[:, :h], s[:, h:], r[:, :h], r[:, h:]
        q = jnp.concatenate([sr * rr - si * ri, sr * ri + si * rr], axis=1)
        q_v[...] = q.astype(bf16)
        t = t_v[...]
        coef = -jax.nn.sigmoid(-jnp.sum(q * t, axis=1, keepdims=True))
        dq[...] = coef * t
        return exact_dot(at_t[k], coef * q)

    def group(k, o):
        at = hop(z_lo, 4 - o)
        block = negs[k, at].reshape(4 * n, 256)
        qb = q_v[...]
        scores = lax.dot_general(qb, block, (((1,), (1,)), ((), ())), preferred_element_type=f32)
        gb = (jax.nn.sigmoid(scores) * (1.0 / (16 * n))).astype(bf16)
        dn = lax.dot_general(gb, qb, (((0,), (0,)), ((), ())), preferred_element_type=f32)
        dn_f[k, at] = dn.reshape(4, n, 256)
        dn_b[k, at] = dn.astype(bf16).reshape(4, n, 256)
        for p in (1, 2, 3):
            to = hop(y, p)
            send(k, RS_Y + 3 * o + p - 1, dn_b.at[k, at, to], rs_y.at[k, at, p], device(y_=to))
        dq[...] += jnp.dot(gb, block, preferred_element_type=f32)

    def scatter_y(k):
        for o in (1, 2, 3, 0):
            at = hop(z_lo, 4 - o)
            total = dn_f[k, at, y]
            for p in (1, 2, 3):
                recv(k, RS_Y + 3 * o + p - 1, rs_y.at[k, at, p])
                total = total + rs_y[k, at, p].astype(f32)
            if o:
                z_b[k, o] = total.astype(bf16)
                send(k, RS_Z + o - 1, z_b.at[k, o], rs_z.at[k, o], z_line(4 - o))
            else:
                own = total
        return own

    def scatter_z(k, total):
        for o in (1, 2, 3):
            recv(k, RS_Z + o - 1, rs_z.at[k, o])
            total = total + rs_z[k, o].astype(f32)
        return exact_dot(spread(neg_row(k), 256), total)

    def rel_start(k):
        total = exact_dot(at_r[k], back(dq[...], s_v[...]))
        for h in range(2):
            gr[k, h, :rels] = total[:, 128 * h : 128 * h + 128]
            gr[k, h, rels:] = jnp.zeros_like(gr[k, h, rels:])
        send(k, PAIR_A, gr.at[k, 1 - core], pair.at[k], other)

    def finish_s(k):
        g = exact_dot(at_s[k], back(dq[...], r_v[...]))
        s_tab[...], s_st[...] = adagrad(s_tab[...], s_st[...], g)

    def rel_pair(k):
        recv(k, PAIR_A, pair.at[k])
        part[k] = (gr[k, core] + pair[k]).reshape(16, 32, 128)

        def one(o, _):
            p, dev = at_spot(o)
            remote(k, XY_A + o, part.at[k, p], xy.at[k, o], dev).start()
            return 0

        lax.fori_loop(1, 16, one, 0)

    def rel_xy(k):
        total = part[k, spot]
        for o in range(1, 16):
            recv(k, XY_A + o, xy.at[k, o])
            total = total + xy[k, o]
        piece[k] = total.reshape(4, 8, 128)
        zs[k, z] = piece[k, z_lo]

        def one(o, _):
            p, dev = at_z(o)
            remote(k, Z_A + o, piece.at[k, p % 4], zs.at[k, z], dev).start()
            return 0

        lax.fori_loop(1, 16, one, 0)

    def rel_share(k, j, tile):
        def one(o, _):
            remote(k, XY_B + 16 * j + o, tile, tile, at_spot(o)[1]).start()
            return 0

        lax.fori_loop(1, 16, one, 0)

    def rel_z(k):
        for o in range(1, 16):
            recv(k, Z_A + o, zs.at[k, (z + 16 - o) % 16])
        tiles = [zs[k, i] for i in range(16)]
        while len(tiles) > 1:
            tiles = [a + b for a, b in zip(tiles[::2], tiles[1::2])]
        done[k, core, z_lo, spot] = tiles[0]
        own = done.at[k, core, z_lo, spot]
        for o in (1, 2, 3):
            send(k, ZL_B + o - 1, own, own, z_line(o))
        rel_share(k, 0, own)

    def rel_line(k):
        for o in (1, 2, 3):
            got = done.at[k, core, hop(z_lo, 4 - o), spot]
            recv(k, ZL_B + o - 1, got)
            rel_share(k, o, got)

    def rel_back(k):
        for j in range(4):
            at = hop(z_lo, 4 - j)

            def one(o, _):
                recv(k, XY_B + 16 * j + o, done.at[k, core, at, (spot + 16 - o) % 16])
                return 0

            lax.fori_loop(1, 16, one, 0)
            send(k, PAIR_B + j, done.at[k, core, at], done.at[k, core, at], other)

    def rel_update(k):
        for j in range(4):
            recv(k, PAIR_B + j, done.at[k, 1 - core, hop(z_lo, 4 - j)])
        for h in range(2):
            for p in range(16):
                for j in range(4):
                    row = 32 * p + 8 * j
                    if row < rels:
                        g_r[row : row + 8, 128 * h : 128 * h + 128] = done[k, h, j, p]
        return adagrad(r_tab[:rels], r_st[:rels], g_r[...])

    loads[0].wait()
    loads[1].wait()
    my_negs(0, t_in[...])
    n_f[...] = jnp.broadcast_to(jnp.concatenate([neg_row(0), neg_row(0)], axis=1), n_f.shape).astype(f32)
    pl.semaphore_wait(barrier, 31)
    send_negs(0)
    send(0, IDX, n_f, n_got, across)

    for load in loads[2:]:
        load.wait()
    gather_t(0, t_in[...])
    gather_s(0)
    place_edges(0)
    r_tab[rels:] = jnp.zeros_like(r_tab[rels:])
    gather_r(0)
    forward_negs(0)
    t_st[...] = columns(ts_in[...])
    g_t = edges(0)
    soon, state = adagrad(t_in[...], t_st[...], g_t)
    t_soon[...] = soon
    ts_soon[...] = state.T[:8]
    send(0, EARLY, t_soon, t_got, across)
    send(0, EARLY + 1, ts_soon, ts_got, across)
    for o in range(4):
        wait_group(0, o)
        group(0, o)
    rel_start(0)
    s_st[...] = columns(ss_in[...])
    pad = jnp.concatenate([rs_in[...], jnp.ones((1, 512 - rels), f32)], axis=1)
    r_st[...] = columns(pad)
    rel_pair(0)
    own = scatter_y(0)
    finish_s(0)
    rel_xy(0)
    new, state = adagrad(t_in[...], t_st[...], g_t + scatter_z(0, own))
    row = jnp.concatenate([neg_row(0), neg_row(0)], axis=1)
    ones = pick(columns(row)[:n], 256)
    high, rest = split2(new)
    low = (new - high.astype(f32) - rest.astype(f32)).astype(bf16)
    wide = jnp.dot(ones, jnp.concatenate([high, rest, low], axis=1), preferred_element_type=f32)
    late[...] = wide[:, :256] + wide[:, 256:512] + wide[:, 512:]
    late_st[...] = state.T[:8]
    send(0, LATE, late, late_got, across)
    send(0, LATE + 1, late_st, late_st_got, across)
    place_edges(1)
    gather_s(1)
    recv(0, IDX, n_got)
    row = n_got[:1, :].astype(i32)
    col = columns(row)
    lane = lax.broadcasted_iota(i32, col.shape, 1)
    before = lax.broadcasted_iota(i32, col.shape, 0) < lane
    again = jnp.max(jnp.where(before & (col == row), 1.0, 0.0), axis=0, keepdims=True)
    row = row[:, :n]
    hits = jnp.where(lax.broadcasted_iota(i32, (256, n), 0) == row, 1.0, 0.0)
    first = (hits * (1.0 - again[:, :n])).astype(bf16)
    hit = jnp.max(hits, axis=1, keepdims=True) > 0.5
    recv(0, EARLY, t_got)
    recv(0, EARLY + 1, ts_got)
    recv(0, LATE, late_got)
    recv(0, LATE + 1, late_st_got)
    x_late = late_got[...]
    high, rest = split2(x_late)
    low = (x_late - high.astype(f32) - rest.astype(f32)).astype(bf16)
    wide = jnp.dot(first, jnp.concatenate([high, rest, low], axis=1), preferred_element_type=f32)
    t_tab[...] = jnp.where(hit, wide[:, :256] + wide[:, 256:512] + wide[:, 512:], t_got[...])
    my_negs(1, t_tab[...])
    send_negs(1)
    rel_z(0)
    t_st[...] = jnp.where(hit, columns(late_st_got[:1, :]), columns(ts_got[:1, :]))
    gather_t(1, t_tab[...])
    forward_negs(1)
    rel_line(0)
    rel_back(0)
    r_tab[:rels], r_st[:rels] = rel_update(0)

    gather_r(1)
    g_t = edges(1)
    for o in range(4):
        wait_group(1, o)
        group(1, o)
    rel_start(1)
    rel_pair(1)
    own = scatter_y(1)
    finish_s(1)
    ss_out[...] = s_st[...].T[:1]
    rel_xy(1)
    t_out[...], state = adagrad(t_tab[...], t_st[...], g_t + scatter_z(1, own))
    ts_out[...] = state.T[:1]
    rel_z(1)
    rel_line(1)
    rel_back(1)
    r_out[...], state = rel_update(1)
    r_st[:rels] = state
    rs_out[...] = r_st[...].T[:1, :rels]

    for copy in waits:
        copy.wait_send()
    for k in range(2):
        def one(o, _):
            p, dev = at_spot(o)
            remote(k, XY_A + o, part.at[k, p], xy.at[k, o], dev).wait_send()
            remote(k, Z_A + o, piece.at[k, z_lo], zs.at[k, z], at_z(o)[1]).wait_send()
            for j in range(4):
                own = done.at[k, core, z_lo, spot]
                remote(k, XY_B + 16 * j + o, own, own, dev).wait_send()
            return 0

        lax.fori_loop(1, 16, one, 0)


def shards(src_table, src_state, dst_table, dst_state, relations, rel_state, src_rows, dst_rows, rel_ids, neg_rows):
    rows, d = src_table.shape
    rels, edges, n = relations.shape[0], src_rows.shape[1], neg_rows.shape[1]
    vm = pltpu.VMEM
    shapes = [
        jax.ShapeDtypeStruct((rows, d), f32),
        jax.ShapeDtypeStruct((1, rows), f32),
        jax.ShapeDtypeStruct((rows, d), f32),
        jax.ShapeDtypeStruct((1, rows), f32),
        jax.ShapeDtypeStruct((rels, d), f32),
        jax.ShapeDtypeStruct((1, rels), f32),
    ]
    out = pl.pallas_call(
        kernel,
        out_shape=shapes,
        in_specs=[pl.BlockSpec(memory_space=pltpu.HBM)] * 10,
        out_specs=[pl.BlockSpec(memory_space=vm)] * 6,
        scratch_shapes=[
            vm((1, rows), f32),
            vm((rows, d), f32),
            vm((1, rows), f32),
            vm((512, d), f32),
            vm((1, rels), f32),
            vm((2, edges), i32),
            vm((2, edges), i32),
            vm((2, edges), i32),
            vm((2, n), i32),
            vm((2, 4, 4, n, d), bf16),
            vm((2, 4, 4, n, d), f32),
            vm((2, 4, 4, n, d), bf16),
            vm((2, 4, 4, n, d), bf16),
            vm((2, 4, n, d), bf16),
            vm((2, 4, n, d), bf16),
            vm((8, 2 * n), f32),
            vm((8, 2 * n), f32),
            vm((rows, d), f32),
            vm((8, rows), f32),
            vm((rows, d), f32),
            vm((8, rows), f32),
            vm((n, d), f32),
            vm((8, rows), f32),
            vm((n, d), f32),
            vm((8, rows), f32),
            vm((2, 2, 512, 128), f32),
            vm((2, 512, 128), f32),
            vm((2, 16, 32, 128), f32),
            vm((2, 16, 32, 128), f32),
            vm((2, 4, 8, 128), f32),
            vm((2, 16, 8, 128), f32),
            vm((2, 2, 4, 16, 8, 128), f32),
            vm((rows, 128), f32),
            vm((rows, 128), f32),
            vm((rows, d), f32),
            vm((512, 128), f32),
            vm((2, rows, edges), bf16),
            vm((2, rows, edges), bf16),
            vm((2, rels, edges), bf16),
            vm((2, edges, 512), bf16),
            vm((rels, d), f32),
            vm((edges, d), bf16),
            vm((edges, d), f32),
            vm((edges, d), f32),
            vm((edges, d), f32),
            vm((edges, d), f32),
            pltpu.SemaphoreType.DMA((10,)),
            pltpu.SemaphoreType.DMA((2, SEMS)),
            pltpu.SemaphoreType.DMA((2, SEMS)),
        ],
        compiler_params=pltpu.CompilerParams(
            collective_id=0, has_side_effects=True, vmem_limit_bytes=62500000
        ),
    )(
        src_table, src_state.reshape(1, rows), dst_table, dst_state.reshape(1, rows),
        relations, rel_state.reshape(1, rels), src_rows, dst_rows, rel_ids, neg_rows,
    )
    s, ss, t, ts, r, rs = out
    return s, ss.reshape(rows), t, ts.reshape(rows), r, rs.reshape(rels)


def solution(mesh):
    both = ("dom", "cuts")
    return jax.shard_map(
        shards,
        mesh=mesh,
        in_specs=(P(both, None), P(both), P(both, None), P(both), P(), P()) + (P(None, both),) * 4,
        out_specs=(P(both, None), P(both), P(both, None), P(both), P(), P()),
        check_vma=False,
    )
```

time: 116 us -> 99.8 us (0.86)
  Pallas kernels: 105 us -> 94.1 us
  local copies, waits for them, and re-layouts: 9.6 us -> 4.91 us
    pallas_call x1, Pallas kernels: 105 us -> 94.1 us  [shards(): pl.pallas_call(kernel, out_shape=shapes, in_specs=[pl.BlockSpec(memory_sp...]
    unnamed x24 -> x16, local copies, waits for them, and re-layouts: 8.82 us -> 4.91 us
where the time goes in v2:
time: 99.8 us; the launch traced here: 99.7 us
  Pallas kernels  94.1 us (94%)
  local copies, waits for them, and re-layouts  4.91 us (5%)
    pallas_call x1, Pallas kernels, shards(): pl.pallas_call(kernel, out_shape=shapes, in_specs=[pl.BlockSpec(memory_sp...  94.1 us
    unnamed x16, local copies, waits for them, and re-layouts  4.91 us

profile of v2, /device:TPU:1, one launch (start us, length us, event | category | flops | bytes accessed | tf_op | source)
XLA Modules:
  0.0 99.7 jit_solution(12898705406716192068)
XLA Ops:
  0.6 94.1 %shard_map.145 = (f32[256,256]{1,0:T(8,128)}, f32[1,256]{1,0:T(1,128)}, f32[256,256]{1,0:T(8,128)}, f32[1,256]{1,0:T(1,128)}, f32[400,256]{1,0:T(8,128)}, /*index=5*/f32[1,400]{1,0:T(1,128)}) custom-call(f32[256,256]{1,0:T(8,128)} %s_hbm.1, f32[1,256]{1,0:T(1,128)} %bitcast.8, f32[256,256]{1,0:T(8,128)} %t_hbm.1, f32[1,256]{1,0:T(1,128)} %bitcast.9, ...), custom_call_target="tpu_custom_call" | custom-call | tf_op jit(solution)/shard_map/pallas_call | solution.py:427
  94.7 0.0 copy-start.4
  94.7 0.0 copy-start.1
  94.7 0.0 copy-start
  94.7 1.7 %copy.22 = f32[256,256]{1,0:T(8,128)} copy(f32[256,256]{1,0:T(8,128)} %get-tuple-element.24) | data formatting | bytes 524288
  96.5 0.0 copy-done.4
  96.5 0.6 copy.23
  97.0 0.0 copy-done.1
  97.0 0.0 copy-start.3
  97.0 0.7 copy.24
  97.8 0.0 copy-done.3
  97.8 0.6 copy.25
  98.3 0.0 copy-done
  98.3 0.0 copy-start.2
  98.3 0.8 copy.26
  99.1 0.0 copy-done.2
  99.1 0.6 copy.27
Async XLA Ops:
  94.7 1.8 %copy-start.4 = (f32[1,256]{1,0:T(1,128)S(1)}, f32[1,256]{1,0:T(1,128)}, u32[]{:S(2)}) copy-start(f32[1,256]{1,0:T(1,128)} %get-tuple-element.13) | copy-start | bytes 3076
  94.7 2.3 %copy-start.1 = (f32[256,256]{1,0:T(8,128)S(1)}, f32[256,256]{1,0:T(8,128)}, u32[]{:S(2)}) copy-start(f32[256,256]{1,0:T(8,128)} %get-tuple-element.26) | copy-start | bytes 786436
  94.7 3.6 %copy-start = (f32[400,256]{1,0:T(8,128)S(1)}, f32[400,256]{1,0:T(8,128)}, u32[]{:S(2)}) copy-start(f32[400,256]{1,0:T(8,128)} %get-tuple-element.28) | copy-start | bytes 1228804
  97.0 0.7 copy-start.3
  98.3 0.8 copy-start.2
